TPU v7x, 512 devices: a whole 4x8x8 slice. The times are simulated.
512 devices in a mesh: ctx: 64 (over x, y_hi, z), tp: 8 (over y_lo, core).
Axes of the slice: x: 4, y: 8 (y_hi: 2, y_lo: 4; y = y_hi * 4 + y_lo), z: 8, core: 2. Of those that a mesh axis runs over, the one named last changes fastest.
Arguments:
- inputs: float32 [64, 2, 64, 2048], P('ctx', None, None, 'tp'), may hold values from -0.3 to 0.3
- b_matrix: float32 [64, 2, 64, 1024], P('ctx', None, None, 'tp'), may hold values from -1.2 to 1.2
- c_matrix: float32 [64, 2, 64, 1024], P('ctx', None, None, 'tp'), may hold values from -1.2 to 1.2
- step_sizes: float32 [64, 2, 64, 64], P('ctx', None, 'tp'), may hold values from 0.3 to 8192, as said below
- decay_rate: float32 [64], P('tp'), as said below
- cotangent: float32 [64, 2, 64, 2048], P('ctx', None, None, 'tp'), may hold values from -7.5 to 7.5
Outputs:
- grad_inputs: float32 [64, 2, 64, 2048], P('ctx', None, None, 'tp')
- grad_b: float32 [64, 2, 64, 1024], P('ctx', None, None, 'tp')
- grad_c: float32 [64, 2, 64, 1024], P('ctx', None, None, 'tp')
- grad_steps: float32 [64, 2, 64, 64], P('ctx', None, 'tp')
Inputs may be any that keep to these rules, and one draw needn't show every extreme that they name: `decay_rate`: each head's rate is positive. `step_sizes`: steps are positive.
All inputs are finite; a program needn't handle non-finite values.
Results may differ from a plain program's by a relative error of at most 0.0003.
Values sent between devices are 32-bit elements; how exact they have to be, the bound alone decides.
A program may use at most 128 MiB of HBM per device.

v0:
```python
import jax
import jax.numpy as jnp
from jax import lax
from jax.sharding import PartitionSpec as P

HEAD_DIM = 32
STATE = 128


HIGHEST = lax.Precision.HIGHEST


def entering_2(array, axis, combine, identity, reverse):
    peers, mine = (lax.axis_size(axis), lax.axis_index(axis))
    everything = jax.tree.map(lambda part: lax.all_gather(part, axis), array)
    start = jax.tree.map(
        lambda part, zero: jnp.broadcast_to(jnp.asarray(zero, part.dtype), part.shape),
        array,
        identity,
    )

    def step(k, before):
        at = peers - 1 - k if reverse else k
        reached = at > mine if reverse else at < mine
        new = combine(before, jax.tree.map(lambda part: part[at], everything))
        return jax.tree.map(lambda a, b: jnp.where(reached, a, b), new, before)

    return lax.fori_loop(0, peers, step, start)


def half_pass(inputs_h, b_block, c_block, step_block, decay_rate, state_in):
    head_count = step_block.shape[0]
    length = step_block.shape[1]
    head_width = state_in.shape[1]
    state_width = state_in.shape[2]
    group_count = b_block.shape[1] // state_width
    per_group = head_count // group_count
    log_decay = -decay_rate[:, None] * step_block
    cumulative = jnp.cumsum(log_decay, axis=1)
    row_ids = lax.broadcasted_iota(jnp.int32, (length, length), 0)
    col_ids = lax.broadcasted_iota(jnp.int32, (length, length), 1)
    causal = row_ids >= col_ids
    b_three = b_block.reshape(length, group_count, state_width)
    c_three = c_block.reshape(length, group_count, state_width)
    scores = jnp.einsum("tgn,sgn->gts", c_three, b_three, precision=HIGHEST)
    decays = jnp.exp(
        jnp.where(causal[None], cumulative[:, :, None] - cumulative[:, None, :], -jnp.inf)
    )
    weights = scores[:, None] * decays.reshape(group_count, per_group, length, length)
    per_head = inputs_h.reshape(length, group_count, per_group, head_width)
    inner_portion = jnp.einsum("gkts,sgkp->tgkp", weights, per_head, precision=HIGHEST)
    state_four = state_in.reshape(group_count, per_group, head_width, state_width)
    growth = jnp.exp(cumulative).T.reshape(length, group_count, per_group, 1)
    carried = jnp.einsum("tgn,gkpn->tgkp", c_three, state_four, precision=HIGHEST) * growth
    to_end = jnp.exp(cumulative[:, -1:] - cumulative).T.reshape(length, group_count, per_group, 1)
    weighted = per_head * to_end
    fresh = jnp.einsum("sgkp,sgn->gkpn", weighted, b_three, precision=HIGHEST).reshape(
        head_count, head_width, state_width
    )
    state_out = jnp.exp(cumulative[:, -1])[:, None, None] * state_in + fresh
    return ((inner_portion + carried).reshape(length, head_count * head_width), state_out)


def summaries(inputs_h, b_block, c_block, step_block, decay_rate, cotan_block, head_width):
    head_count = step_block.shape[0]
    length = step_block.shape[1]
    state_width = STATE
    group_count = b_block.shape[1] // state_width
    per_group = head_count // group_count
    cumulative = jnp.cumsum(-decay_rate[:, None] * step_block, axis=1)
    total = jnp.exp(cumulative[:, -1])
    b_three = b_block.reshape(length, group_count, state_width)
    c_three = c_block.reshape(length, group_count, state_width)
    per_head = inputs_h.reshape(length, group_count, per_group, head_width)
    to_end = jnp.exp(cumulative[:, -1:] - cumulative).T.reshape(length, group_count, per_group, 1)
    state_zero = jnp.einsum(
        "sgkp,sgn->gkpn", per_head * to_end, b_three, precision=HIGHEST
    ).reshape(head_count, head_width, state_width)
    cotan_head = cotan_block.reshape(length, group_count, per_group, head_width)
    from_start = jnp.exp(cumulative).T.reshape(length, group_count, per_group, 1)
    adjoint_zero = jnp.einsum(
        "tgkp,tgn->gkpn", cotan_head * from_start, c_three, precision=HIGHEST
    ).reshape(head_count, head_width, state_width)
    return (total, state_zero, adjoint_zero)


def compose(earlier, later):
    return (earlier[0] * later[0], later[0][:, None, None] * earlier[1] + later[1])


def per_device(inputs, b_matrix, c_matrix, step_sizes, decay_rate, cotangent):
    total_first, hidden_opening, adjoint_first = summaries(
        inputs[0, 0],
        b_matrix[0, 0],
        c_matrix[0, 0],
        step_sizes[0, 0],
        decay_rate,
        cotangent[0, 0],
        HEAD_DIM,
    )
    total_second, state_second, adjoint_second = summaries(
        inputs[0, 1],
        b_matrix[0, 1],
        c_matrix[0, 1],
        step_sizes[0, 1],
        decay_rate,
        cotangent[0, 1],
        HEAD_DIM,
    )
    unit = (jnp.ones_like(total_first), jnp.zeros_like(hidden_opening))
    up_decay_s, upward_state = entering_2(
        (total_first, hidden_opening), "ctx", compose, unit, False
    )
    up_decay_a, up_adjoint = entering_2((total_second, adjoint_second), "ctx", compose, unit, False)
    middle_state = total_first[:, None, None] * upward_state + hidden_opening
    middle_adjoint = total_second[:, None, None] * up_adjoint + adjoint_second
    is_last = lax.axis_index("ctx") == lax.axis_size("ctx") - 1
    seed_state = jnp.where(is_last, middle_state, 0.0)
    seed_adjoint = jnp.where(is_last, middle_adjoint, 0.0)
    down_state_part = state_second + total_second[:, None, None] * seed_state
    down_adjoint_part = adjoint_first + total_first[:, None, None] * seed_adjoint
    down_decay_s, down_state = entering_2(
        (total_second, down_state_part), "ctx", compose, unit, True
    )
    down_decay_a, downward_adjoint = entering_2(
        (total_first, down_adjoint_part), "ctx", compose, unit, True
    )
    entering = (upward_state, down_state + down_decay_s[:, None, None] * seed_state)
    leaving = (downward_adjoint + down_decay_a[:, None, None] * seed_adjoint, up_adjoint)
    grads_x = []
    grads_b = []
    grads_c = []
    grads_s = []
    for half_idx in range(2):
        state_in = entering[half_idx]

        def local_pass(x_block, b_block, c_block, step_block):
            return half_pass(x_block, b_block, c_block, step_block, decay_rate, state_in)

        _, pullback = jax.vjp(
            local_pass,
            inputs[0, half_idx],
            b_matrix[0, half_idx],
            c_matrix[0, half_idx],
            step_sizes[0, half_idx],
        )
        grad_x_half, grad_b_half, grad_c_half, grad_s_half = pullback(
            (cotangent[0, half_idx], leaving[half_idx])
        )
        grads_x.append(grad_x_half)
        grads_b.append(grad_b_half)
        grads_c.append(grad_c_half)
        grads_s.append(grad_s_half)
    grad_inputs = jnp.stack(grads_x)[None]
    grad_steps = jnp.stack(grads_s)[None]
    grad_b = jnp.stack(grads_b)[None]
    grad_c = jnp.stack(grads_c)[None]
    return (grad_inputs, grad_b, grad_c, grad_steps)


def solution(mesh):
    return jax.shard_map(
        per_device,
        mesh=mesh,
        in_specs=(
            P("ctx", None, None, "tp"),
            P("ctx", None, None, "tp"),
            P("ctx", None, None, "tp"),
            P("ctx", None, "tp", None),
            P("tp"),
            P("ctx", None, None, "tp"),
        ),
        out_specs=(
            P("ctx", None, None, "tp"),
            P("ctx", None, None, "tp"),
            P("ctx", None, None, "tp"),
            P("ctx", None, "tp", None),
        ),
        check_vma=False,
    )
```

profile of v0, /device:TPU:1, one launch (start us, length us, event | category | flops | bytes accessed | tf_op | source)
XLA Modules:
  0.0 918.0 jit_solution(2048569665129924316)
XLA Ops:
  10.0 1.7 fusion.39
  13.2 1.6 fusion.45
  15.2 1.3 dynamic-slice
  17.6 209.1 %all-reduce.6 = (f32[512]{0:T(512)S(1)}, f32[512]{0:T(512)S(1)}) all-reduce(f32[512]{0:T(512)S(1)} %dynamic-update-slice.1, f32[512]{0:T(512)S(1)} %dynamic-update-slice), channel_id=3, replica_groups=mesh['ctx'=64,'tp'=8] {'ctx'}, use_global_device_ids=true, to_apply=%add.5 | all-reduce | flops 1024 | bytes 8192
  227.0 66.3 %while.64 = (s32[]{:T(128)}, f32[8,32,128]{2,1,0:T(8,128)S(1)}, s32[]{:T(128)}, f32[64,8]{1,0:T(8,128)S(1)}, f32[64,8,32,128]{3,2,1,0:T(8,128)}, /*index=5*/s32[]{:T(128)}, s32[]{:T(128)}) while((s32[]{:T(128)}, f32[8,32,128]{2,1,0:T(8,128)S(1)}, s32[]{:T(128)}, f32[64,8]{1,0:T(8,128)S(1)}, f32[64,8,32,128]{3,2,1,0:T(8,128)}, ...), condition=%wide.region_3.4_spmd.clone, body=%wide.region_2.3_spmd.clone.sunk | while | flops 131076 | bytes 393417 | solution.py:28
  237.4 1.0 fusion.119
  239.5 1.0 fusion.119
  264.3 1.0 fusion.119
  272.6 1.0 fusion.119
  273.6 1.0 fusion.119
  278.8 1.0 fusion.119
  285.0 1.0 fusion.119
  288.1 1.0 fusion.119
  293.3 1.0 multiply_reduce_fusion.2
  294.6 102.4 %all-gather.15.cloned.1.call-done = f32[512,32,128]{2,1,0:T(8,128)} async-done(((f32[8,32,128]{2,1,0:T(8,128)}), f32[512,32,128]{2,1,0:T(8,128)}) %all-gather.15.cloned.1.call-update) | async-done | bytes 8388624 | tf_op jit(solution)/shard_map/all_gather | solution.py:15
  397.0 66.1 %while.66 = (s32[]{:T(128)}, f32[8,32,128]{2,1,0:T(8,128)S(1)}, s32[]{:T(128)}, f32[64,8]{1,0:T(8,128)S(1)}, f32[64,8,32,128]{3,2,1,0:T(8,128)}, /*index=5*/s32[]{:T(128)}, s32[]{:T(128)}) while((s32[]{:T(128)}, f32[8,32,128]{2,1,0:T(8,128)S(1)}, s32[]{:T(128)}, f32[64,8]{1,0:T(8,128)S(1)}, f32[64,8,32,128]{3,2,1,0:T(8,128)}, ...), condition=%wide.region_9.10_spmd.clone, body=%wide.region_8.9_spmd.clone.sunk | while | flops 131076 | bytes 393417 | solution.py:28
  463.1 1.8 convolution_add_fusion
  470.3 179.0 %all-gather.17.cloned.1.call-done = f32[512,32,128]{2,1,0:T(8,128)} async-done(((f32[8,32,128]{2,1,0:T(8,128)}), f32[512,32,128]{2,1,0:T(8,128)}) %all-gather.17.cloned.1.call-update) | async-done | bytes 8388624 | tf_op jit(solution)/shard_map/all_gather | solution.py:15
  649.3 67.1 %while.67 = (s32[]{:T(128)}, f32[8]{0:T(128)S(1)}, f32[8,32,128]{2,1,0:T(8,128)S(1)}, s32[]{:T(128)}, f32[64,8]{1,0:T(8,128)S(1)}, /*index=5*/f32[64,8,32,128]{3...) while((s32[]{:T(128)}, f32[8]{0:T(128)S(1)}, f32[8,32,128]{2,1,0:T(8,128)S(1)}, ...), condition=%wide.region_11.12_spmd.clone, body=%wide.region_10.11_spmd.clone.sunk | while | flops 131104 | bytes 393553 | solution.py:28
  650.4 1.0 fusion.122
  651.4 1.0 fusion.122
  652.5 1.0 fusion.122
  653.5 1.0 fusion.122
  654.6 1.0 fusion.122
  655.6 1.0 fusion.122
  656.7 1.0 fusion.122
  657.7 1.0 fusion.122
  658.8 1.0 fusion.122
  659.8 1.0 fusion.122
  660.9 1.0 fusion.122
  661.9 1.0 fusion.122
  663.0 1.0 fusion.122
  664.0 1.0 fusion.122
  665.1 1.0 fusion.122
  666.1 1.0 fusion.122
  667.2 1.0 fusion.122
  668.2 1.0 fusion.122
  669.3 1.0 fusion.122
  674.5 1.0 fusion.122
  676.6 1.0 fusion.122
  677.7 1.0 fusion.122
  678.7 1.0 fusion.122
  679.8 1.0 fusion.122
  687.1 1.0 fusion.122
  689.2 1.0 fusion.122
  706.0 1.0 fusion.122
  716.5 122.0 %all-gather.13.cloned.1.call-done = f32[512,32,128]{2,1,0:T(8,128)} async-done(((f32[8,32,128]{2,1,0:T(8,128)}), f32[512,32,128]{2,1,0:T(8,128)}) %all-gather.13.cloned.1.call-update) | async-done | bytes 8388624 | tf_op jit(solution)/shard_map/all_gather | solution.py:15
  838.5 67.2 %while.65 = (s32[]{:T(128)}, f32[8]{0:T(128)S(1)}, f32[8,32,128]{2,1,0:T(8,128)S(1)}, s32[]{:T(128)}, f32[64,8]{1,0:T(8,128)S(1)}, /*index=5*/f32[64,8,32,128]{3...) while((s32[]{:T(128)}, f32[8]{0:T(128)S(1)}, f32[8,32,128]{2,1,0:T(8,128)S(1)}, ...), condition=%wide.region_5.6_spmd.clone, body=%wide.region_4.5_spmd.clone.sunk | while | flops 131104 | bytes 393553 | solution.py:28
  (567 shorter events, 239.9 us)
Async XLA Ops:
  7.2 458.0 %copy-start.2 = (f32[1,2,64,128]{3,2,1,0:T(8,128)S(1)}, f32[1,2,64,128]{3,2,1,0:T(8,128)}, u32[]{:S(2)}) copy-start(f32[1,2,64,128]{3,2,1,0:T(8,128)} %param.16) | copy-start | bytes 196612
  7.2 455.9 %copy-start.3 = (f32[1,2,64,128]{3,2,1,0:T(8,128)S(1)}, f32[1,2,64,128]{3,2,1,0:T(8,128)}, u32[]{:S(2)}) copy-start(f32[1,2,64,128]{3,2,1,0:T(8,128)} %param.15) | copy-start | bytes 196612
  7.2 219.8 %all-gather.11.cloned.1.call-start = ((), (), s32[]{:S(2)}) async-start(), calls=%async_computation | async-start | bytes 8519680 | tf_op jit(solution)/shard_map/all_gather | solution.py:15
  11.6 457.7 %copy-start = (f32[8,32,128]{2,1,0:T(8,128)S(1)}, f32[8,32,128]{2,1,0:T(8,128)}, u32[]{:S(2)}) copy-start(f32[8,32,128]{2,1,0:T(8,128)} %fusion.39) | copy-start | bytes 393220
  11.6 385.3 %all-gather.15.cloned.1.call-start = ((), (), s32[]{:S(2)}) async-start(), calls=%async_computation.2 | async-start | bytes 8519680 | tf_op jit(solution)/shard_map/all_gather | solution.py:15
  14.9 890.8 %copy-start.1 = (f32[8,32,128]{2,1,0:T(8,128)S(1)}, f32[8,32,128]{2,1,0:T(8,128)}, u32[]{:S(2)}) copy-start(f32[8,32,128]{2,1,0:T(8,128)} %fusion.45) | copy-start | bytes 393220
  14.9 634.4 %all-gather.17.cloned.1.call-start = ((), (), s32[]{:S(2)}) async-start(), calls=%async_computation.3 | async-start | bytes 8519680 | tf_op jit(solution)/shard_map/all_gather | solution.py:15
  464.9 373.5 %all-gather.13.cloned.1.call-start = ((), (), s32[]{:S(2)}) async-start(), calls=%async_computation.1 | async-start | bytes 8519680 | tf_op jit(solution)/shard_map/all_gather | solution.py:15
Sparse Core Ops, SparseCore 0:
  13.1 196.1 all-gather.10
  213.8 183.0 all-gather.14
  465.1 184.2 all-gather.16
  654.3 184.1 all-gather.12
where the time goes:
time: 925 us; the launch traced here: 918 us
  waiting for transfers between devices  404 us (44%)
  other arithmetic  263 us (28%)
  blocking collectives  209 us (23%)
  between operations  14.8 us (2%)
  matrix products  13 us (1%)
    all_gather x4, waiting for transfers between devices, entering_2(): everything = jax.tree.map(lambda part: lax.all_gather(part, axis), array)  403 us
    select_n x384, other arithmetic, step(): return jax.tree.map(lambda a, b: jnp.where(reached, a, b), new, before)  257 us
    unnamed x1, blocking collectives  209 us
  transfers between devices with their start and end apart: 4, of which 3 were waited for; matrix products, arithmetic and copies ran while one was open for 15% of the time, Pallas kernels for 0%

commit v1 on v0

v1 whole, which is shorter than its diff:
```python
import functools

import jax
import jax.numpy as jnp
from jax import lax
from jax.experimental import pallas as pl
from jax.experimental.pallas import tpu as pltpu
from jax.sharding import PartitionSpec as P

F32 = jnp.float32
BF16 = jnp.bfloat16
HIGHEST = lax.Precision.HIGHEST
MESH = pl.DeviceIdType.MESH

N = 64
T = 64
H = 8
PW = 32
W = H * PW
S = 128

NN = (((1,), (0,)), ((), ()))
NT = (((1,), (1,)), ((), ()))
TN = (((0,), (0,)), ((), ()))


def split(a):
    high = a.astype(BF16)
    low = (a - high.astype(F32)).astype(BF16)
    return high, low


def dot(a, b, dims=NN):
    return lax.dot_general(a, b, dims, preferred_element_type=F32)


def mm(a, b, dims=NN):
    return dot(a[0], b[0], dims) + (dot(a[0], b[1], dims) + dot(a[1], b[0], dims))


def exact(a, b, dims=NN):
    return lax.dot_general(a, b, dims, precision=HIGHEST, preferred_element_type=F32)


def iota(shape, dim):
    return lax.broadcasted_iota(jnp.int32, shape, dim)


def kernel(
    x_ref, b_ref, c_ref, st_ref, rate_ref, g_ref,
    gx_ref, gb_ref, gc_ref, gs_ref,
    dec, decs, tiles, send_s, send_a, recv_s, recv_a, out_s, out_a, in_s, in_a,
    sems, rems,
):
    me = lax.axis_index("ctx")
    px, py, pz = me // 16, (me // 8) % 2, me % 8

    def peer(o):
        dx, dy, dz = o % 4, (o // 4) % 2, o // 8
        return ((px + dx) % 4) * 16 + ((py + dy) % 2) * 8 + (pz + dz) % 8

    barrier = pltpu.get_barrier_semaphore()

    def greet(i, carry):
        pl.semaphore_signal(
            barrier, inc=1, device_id={"ctx": peer(N - 1 - i)}, device_id_type=MESH
        )
        return carry

    lax.fori_loop(0, N - 1, greet, 0, unroll=7)

    def send_all(source, target, which, at):
        def one(i, carry):
            to = peer(N - 1 - i)
            pltpu.make_async_remote_copy(
                src_ref=source.at[at(to)],
                dst_ref=target.at[me],
                send_sem=sems.at[which],
                recv_sem=rems.at[which],
                device_id={"ctx": to},
                device_id_type=MESH,
            ).start()
            return carry

        lax.fori_loop(0, N - 1, one, 0, unroll=7)

    def wait_all(sem, which, like):
        some = like.at[pl.ds(0, N - 1)]
        pltpu.make_async_copy(some, some, sem.at[which]).wait()

    head = iota((H, T), 0)
    rate = jnp.zeros((H, T), F32)
    for h in range(H):
        rate = jnp.where(head == h, rate_ref[h], rate)
    row_t, col_t = iota((T, T), 0), iota((T, T), 1)
    tri = (col_t <= row_t).astype(F32)
    sel32 = (iota((H, W), 1) // PW == iota((H, W), 0)).astype(F32)
    cum, spread, from_start, to_end = [], [], [], []
    for i in range(2):
        logd = -rate * st_ref[0, i]
        total = jnp.exp(jnp.sum(logd, axis=1, keepdims=True))
        for h in range(H):
            dec[h, pl.ds(i, 1), :] = jnp.broadcast_to(total[h : h + 1], (1, S))
        cum_i = exact(tri, logd, NT)
        wide = exact(cum_i, sel32)
        cum.append(cum_i)
        spread.append(wide)
        from_start.append(jnp.exp(wide))
        to_end.append(jnp.exp(wide[T - 1 : T] - wide))
    decs[me] = dec[me // 8]

    low_half = iota((8, S), 0) < 4
    xw, gw, bs, cs, xs, gs = [], [], [], [], [], []

    def pack(first, second, buffer):
        for k in range(N // 2):
            one, two = first[8 * k : 8 * k + 8], second[8 * k : 8 * k + 8]
            buffer[2 * k] = jnp.where(low_half, one, pltpu.roll(two, 4, 0))
            buffer[2 * k + 1] = jnp.where(low_half, pltpu.roll(one, 4, 0), two)

    for i in range(2):
        x, b = x_ref[0, i], b_ref[0, i]
        xs.append(split(x))
        bs.append(split(b))
        xw.append(split(x * to_end[i]))
    state = [mm(xw[i], bs[i], TN) for i in range(2)]
    pack(state[0], state[1], send_s)
    recv_s[me] = send_s[me]

    pl.semaphore_wait(barrier, N - 1)
    send_all(dec, decs, 0, lambda to: to // 8)
    send_all(send_s, recv_s, 1, lambda to: to)

    for i in range(2):
        g, c = g_ref[0, i], c_ref[0, i]
        gs.append(split(g))
        cs.append(split(c))
        gw.append(split(g * from_start[i]))
    adjoint = [mm(gw[i], cs[i], TN) for i in range(2)]
    pack(adjoint[0], adjoint[1], send_a)
    recv_a[me] = send_a[me]
    send_all(send_a, recv_a, 2, lambda to: to)

    lane_head = iota((T, W), 1) // PW
    t_wide, s_wide = iota((T, H * T), 0), iota((T, H * T), 1) % T
    sel64 = (iota((H, H * T), 1) // T == iota((H, H * T), 0)).astype(F32)
    pick = (iota((H * T, H), 0) // T == iota((H * T, H), 1)).astype(BF16)
    pick32 = (iota((W, H), 0) // PW == iota((W, H), 1)).astype(BF16)
    zero = jnp.zeros((), BF16)

    def stacked(parts):
        return [
            jnp.concatenate([jnp.where(lane_head == h, part, zero) for h in range(H)], axis=0)
            for part in parts
        ]

    def twice(parts):
        return [jnp.concatenate([part, part], axis=0) for part in parts]

    def folded(a):
        return a[:, :128] + a[:, 128:256] + (a[:, 256:384] + a[:, 384:])

    def by_head(a, selection):
        high, low = split(a)
        return dot(high, selection) + dot(low, selection)

    def within(i):
        columns = exact(cum[i], sel64)
        row = jnp.sum(jnp.where(t_wide == s_wide, columns, 0.0), axis=0, keepdims=True)
        gap = columns - row
        forward = jnp.exp(jnp.where(s_wide <= t_wide, gap, -1e30))
        backward = jnp.exp(jnp.where(s_wide >= t_wide, -gap, -1e30))
        b_twice, c_twice = twice(bs[i]), twice(cs[i])
        x_stack, g_stack = stacked(xs[i]), stacked(gs[i])
        scores = jnp.concatenate([mm(cs[i], b_twice, NT)] * 4, axis=1)
        scores_back = jnp.concatenate([mm(bs[i], c_twice, NT)] * 4, axis=1)
        inner = forward * mm(gs[i], x_stack, NT)
        inner_back = backward * mm(xs[i], g_stack, NT)
        gc_ref[0, i] = mm(split(folded(inner)), b_twice)
        gb_ref[0, i] = mm(split(folded(inner_back)), c_twice)
        gx_ref[0, i] = mm(split(scores_back * backward), g_stack)
        off = s_wide != t_wide
        return by_head(jnp.where(off, scores * inner, 0.0), pick) - by_head(
            jnp.where(off, scores_back * inner_back, 0.0), pick
        )

    d_cum = [within(0), None]

    def scan(received, result, low_first):
        keep = low_half if low_first else jnp.logical_not(low_half)

        def up(j, carry):
            result[j] = carry
            return tiles[j] * carry + received[j]

        top = lax.fori_loop(0, N, up, jnp.zeros((8, S), F32), unroll=8)

        def down(i, carry):
            j = N - 1 - i
            result[j] = jnp.where(keep, result[j], carry)
            return tiles[j] * carry + received[j]

        lax.fori_loop(0, N, down, pltpu.roll(top, 4, 0), unroll=8)

    wait_all(rems, 0, decs)

    def spread_decay(j, carry):
        tiles[j] = jnp.where(low_half, decs[j, 0:1, :], decs[j, 1:2, :])
        return carry

    lax.fori_loop(0, N, spread_decay, 0, unroll=8)
    wait_all(rems, 1, recv_s)
    scan(recv_s, out_s, True)
    in_s[me] = out_s[me]
    send_all(out_s, in_s, 3, lambda to: to)
    wait_all(rems, 2, recv_a)
    scan(recv_a, out_a, False)
    in_a[me] = out_a[me]
    send_all(out_a, in_a, 4, lambda to: to)

    d_cum[1] = within(1)

    def unpack(buffer):
        first, second = [], []
        for k in range(N // 2):
            one, two = buffer[2 * k], buffer[2 * k + 1]
            first.append(jnp.where(low_half, one, pltpu.roll(two, 4, 0)))
            second.append(jnp.where(low_half, pltpu.roll(one, 4, 0), two))
        return jnp.concatenate(first, axis=0), jnp.concatenate(second, axis=0)

    wait_all(rems, 3, in_s)
    entering = unpack(in_s)
    for i in range(2):
        parts = split(entering[i])
        carried = mm(cs[i], parts, NT)
        gc_ref[0, i] += mm(gw[i], parts)
        d_cum[i] += by_head(g_ref[0, i] * from_start[i] * carried, pick32)
    wait_all(rems, 4, in_a)
    leaving = unpack(in_a)
    after = (row_t >= col_t).astype(F32)
    before = (row_t < col_t).astype(F32)
    for i in range(2):
        parts = split(leaving[i])
        weighted = to_end[i] * mm(bs[i], parts, NT)
        gx_ref[0, i] += weighted
        gb_ref[0, i] += mm(xw[i], parts)
        fresh = by_head(x_ref[0, i] * weighted, pick32)
        ends = exact(sel32, leaving[i] * entering[i])
        through = jnp.sum(ends, axis=1, keepdims=True) * jnp.concatenate(
            [dec[h, pl.ds(i, 1), 0:1] for h in range(H)], axis=0
        )
        d_log = exact(d_cum[i], after, TN) + exact(fresh, before, TN) + through
        gs_ref[0, i] = -rate * d_log

    wait_all(sems, 0, decs)
    wait_all(sems, 1, send_s)
    wait_all(sems, 2, send_a)
    wait_all(sems, 3, out_s)
    wait_all(sems, 4, out_a)


def per_device(inputs, b_matrix, c_matrix, step_sizes, decay_rate, cotangent):
    vmem = pl.BlockSpec(memory_space=pltpu.VMEM)
    smem = pl.BlockSpec(memory_space=pltpu.SMEM)
    chunks = pltpu.VMEM((N, 8, S), F32)
    return pl.pallas_call(
        kernel,
        name="mirrored_scan",
        out_shape=[
            jax.ShapeDtypeStruct(a.shape, F32) for a in (inputs, b_matrix, c_matrix, step_sizes)
        ],
        in_specs=[vmem, vmem, vmem, vmem, smem, vmem],
        out_specs=[vmem] * 4,
        scratch_shapes=[
            pltpu.VMEM((H, 2, S), F32),
            pltpu.VMEM((N, 2, S), F32),
            *[chunks] * 9,
            pltpu.SemaphoreType.DMA((5,)),
            pltpu.SemaphoreType.DMA((5,)),
        ],
        compiler_params=pltpu.CompilerParams(
            collective_id=0, has_side_effects=True, vmem_limit_bytes=40 << 20
        ),
    )(inputs, b_matrix, c_matrix, step_sizes, decay_rate, cotangent)


def solution(mesh):
    blocks = P("ctx", None, None, "tp")
    steps = P("ctx", None, "tp", None)
    return jax.shard_map(
        per_device,
        mesh=mesh,
        in_specs=(blocks, blocks, blocks, steps, P("tp"), blocks),
        out_specs=(blocks, blocks, blocks, steps),
        check_vma=False,
    )
```

time: 925 us -> 59.1 us (0.06)
  waiting for transfers between devices: 404 us -> 0 us
  other arithmetic: 263 us -> 0 us
  blocking collectives: 209 us -> 0 us
  Pallas kernels: 0 us -> 50.8 us
  between operations: 14.8 us -> 0.66 us
  matrix products: 13 us -> 0 us
    all_gather x4 -> x0, waiting for transfers between devices: 403 us -> none  [entering_2(): everything = jax.tree.map(lambda part: lax.all_gather(part, axis), array)]
    select_n x384 -> x0, other arithmetic: 257 us -> none  [step(): return jax.tree.map(lambda a, b: jnp.where(reached, a, b), new, before)]
    unnamed x1 -> x0, blocking collectives: 209 us -> none
    pallas_call x0 -> x1, Pallas kernels: none -> 50.8 us  [per_device(): pl.pallas_call(kernel, name='mirrored_scan', out_shape=[jax.ShapeDtypeStr...]
    dot_general x22 -> x0, matrix products: 13 us -> none  [the longest x2 3.47 us: summaries(): jnp.einsum('sgkp,sgn->gkpn', per_head * to_end, b_three, precision=HIGHEST)]
  transfers between devices with their start and end apart: 4 -> 0, of which waited for: 3 -> 0; matrix products, arithmetic and copies ran while one was open for 15% -> 0% of each run, Pallas kernels for 0% -> 0%
where the time goes in v1:
time: 59.1 us; the launch traced here: 58.8 us
  Pallas kernels  50.8 us (86%)
  local copies, waits for them, and re-layouts  7.34 us (12%)
  between operations  0.66 us (1%)
    pallas_call x1, Pallas kernels, per_device(): pl.pallas_call(kernel, name='mirrored_scan', out_shape=[jax.ShapeDtypeStr...  50.8 us
    unnamed x16, local copies, waits for them, and re-layouts  7.34 us

profile of v1, /device:TPU:1, one launch (start us, length us, event | category | flops | bytes accessed | tf_op | source)
XLA Modules:
  0.0 58.8 jit_solution(7403206842116517109)
XLA Ops:
  0.6 0.0 copy-start
  0.6 0.9 %copy-done = f32[1,2,64,256]{3,2,1,0:T(8,128)S(1)} copy-done((f32[1,2,64,256]{3,2,1,0:T(8,128)S(1)}, f32[1,2,64,256]{3,2,1,0:T(8,128)}, u32[]{:S(2)}) %copy-start) | copy-done | bytes 131096
  1.5 0.0 copy-start.1
  1.5 0.9 %copy-done.1 = f32[1,2,64,256]{3,2,1,0:T(8,128)S(1)} copy-done((f32[1,2,64,256]{3,2,1,0:T(8,128)S(1)}, f32[1,2,64,256]{3,2,1,0:T(8,128)}, u32[]{:S(2)}) %copy-start.1) | copy-done | bytes 131096
  2.4 0.0 copy-start.2
  2.4 0.8 %copy-done.2 = f32[1,2,64,128]{3,2,1,0:T(8,128)S(1)} copy-done((f32[1,2,64,128]{3,2,1,0:T(8,128)S(1)}, f32[1,2,64,128]{3,2,1,0:T(8,128)}, u32[]{:S(2)}) %copy-start.2) | copy-done | bytes 65560
  3.3 0.0 copy-start.3
  3.3 0.8 %copy-done.3 = f32[1,2,64,128]{3,2,1,0:T(8,128)S(1)} copy-done((f32[1,2,64,128]{3,2,1,0:T(8,128)S(1)}, f32[1,2,64,128]{3,2,1,0:T(8,128)}, u32[]{:S(2)}) %copy-start.3) | copy-done | bytes 65560
  4.1 0.0 copy-start.4
  4.1 0.7 %copy-done.4 = f32[1,2,8,64]{3,2,1,0:T(8,128)S(1)} copy-done((f32[1,2,8,64]{3,2,1,0:T(8,128)S(1)}, f32[1,2,8,64]{3,2,1,0:T(8,128)}, u32[]{:S(2)}) %copy-start.4) | copy-done | bytes 4120
  4.8 0.0 copy-start.5
  4.8 0.7 %copy-done.5 = f32[8]{0:T(128)S(1)} copy-done((f32[8]{0:T(128)S(1)}, f32[8]{0:T(128)}, u32[]{:S(2)}) %copy-start.5) | copy-done | bytes 56
  5.5 50.8 %mirrored_scan.1 = (f32[1,2,64,256]{3,2,1,0:T(8,128)S(1)}, f32[1,2,64,128]{3,2,1,0:T(8,128)S(1)}, f32[1,2,64,128]{3,2,1,0:T(8,128)S(1)}, f32[1,2,8,64]{3,2,1,0:T(8,128)S(1)}) custom-call(f32[1,2,64,256]{3,2,1,0:T(8,128)S(1)} %copy-done, f32[1,2,64,128]{3,2,1,0:T(8,128)S(1)} %copy-done.2, f32[1,2,64,128]{3,2,1,0:T(8,128)S(1)} %copy-done.3, ...), custom_call_target="tpu_custom_call" | custom-call | tf_op jit(solution)/shard_map/mirrored_scan/pallas_call | solution.py:266
  56.3 0.7 %copy.14 = f32[1,2,64,256]{3,2,1,0:T(8,128)} copy(f32[1,2,64,256]{3,2,1,0:T(8,128)S(1)} %get-tuple-element.8) | data formatting | bytes 262144
  56.9 0.6 %copy.15 = f32[1,2,64,128]{3,2,1,0:T(8,128)} copy(f32[1,2,64,128]{3,2,1,0:T(8,128)S(1)} %get-tuple-element.9) | data formatting | bytes 131072
  57.6 0.6 %copy.16 = f32[1,2,64,128]{3,2,1,0:T(8,128)} copy(f32[1,2,64,128]{3,2,1,0:T(8,128)S(1)} %get-tuple-element.10) | data formatting | bytes 131072
  58.2 0.6 %copy.17 = f32[1,2,8,64]{3,2,1,0:T(8,128)} copy(f32[1,2,8,64]{3,2,1,0:T(8,128)S(1)} %get-tuple-element.11) | data formatting | bytes 8192
Async XLA Ops:
  0.6 0.9 %copy-start = (f32[1,2,64,256]{3,2,1,0:T(8,128)S(1)}, f32[1,2,64,256]{3,2,1,0:T(8,128)}, u32[]{:S(2)}) copy-start(f32[1,2,64,256]{3,2,1,0:T(8,128)} %x_ref.1) | copy-start | bytes 393220
  1.5 0.9 %copy-start.1 = (f32[1,2,64,256]{3,2,1,0:T(8,128)S(1)}, f32[1,2,64,256]{3,2,1,0:T(8,128)}, u32[]{:S(2)}) copy-start(f32[1,2,64,256]{3,2,1,0:T(8,128)} %g_ref.1) | copy-start | bytes 393220
  2.4 0.8 %copy-start.2 = (f32[1,2,64,128]{3,2,1,0:T(8,128)S(1)}, f32[1,2,64,128]{3,2,1,0:T(8,128)}, u32[]{:S(2)}) copy-start(f32[1,2,64,128]{3,2,1,0:T(8,128)} %b_ref.1) | copy-start | bytes 196612
  3.3 0.8 %copy-start.3 = (f32[1,2,64,128]{3,2,1,0:T(8,128)S(1)}, f32[1,2,64,128]{3,2,1,0:T(8,128)}, u32[]{:S(2)}) copy-start(f32[1,2,64,128]{3,2,1,0:T(8,128)} %c_ref.1) | copy-start | bytes 196612
  4.1 0.7 %copy-start.4 = (f32[1,2,8,64]{3,2,1,0:T(8,128)S(1)}, f32[1,2,8,64]{3,2,1,0:T(8,128)}, u32[]{:S(2)}) copy-start(f32[1,2,8,64]{3,2,1,0:T(8,128)} %st_ref.1) | copy-start | bytes 12292
  4.8 0.7 %copy-start.5 = (f32[8]{0:T(128)S(1)}, f32[8]{0:T(128)}, u32[]{:S(2)}) copy-start(f32[8]{0:T(128)} %rate_ref.1) | copy-start | bytes 100

commit v2 on v1

--- a/solution.py
+++ b/solution.py
@@ -47,47 +47,59 @@
 
 
 def kernel(
+    x_any, b_any, c_any, st_any, rate_any, g_any,
+    gx_ref, gb_ref, gc_ref, gs_ref,
     x_ref, b_ref, c_ref, st_ref, rate_ref, g_ref,
-    gx_ref, gb_ref, gc_ref, gs_ref,
     dec, decs, tiles, send_s, send_a, recv_s, recv_a, out_s, out_a, in_s, in_a,
-    sems, rems,
+    sems, rems, loads,
 ):
     me = lax.axis_index("ctx")
     px, py, pz = me // 16, (me // 8) % 2, me % 8
-
-    def peer(o):
-        dx, dy, dz = o % 4, (o // 4) % 2, o // 8
-        return ((px + dx) % 4) * 16 + ((py + dy) % 2) * 8 + (pz + dz) % 8
+    x_part = [lax.rem(px + k, 4) * 16 for k in range(4)]
+    y_part = [lax.rem(py + k, 2) * 8 for k in range(2)]
+    z_part = [lax.rem(pz + k, 8) for k in range(8)]
+    peers = [
+        x_part[x] + y_part[y] + z_part[z]
+        for z in (4, 3, 5, 2, 6, 1, 7, 0)
+        for y in (1, 0)
+        for x in (2, 1, 3, 0)
+    ][:-1]
 
     barrier = pltpu.get_barrier_semaphore()
 
-    def greet(i, carry):
-        pl.semaphore_signal(
-            barrier, inc=1, device_id={"ctx": peer(N - 1 - i)}, device_id_type=MESH
-        )
-        return carry
-
-    lax.fori_loop(0, N - 1, greet, 0, unroll=7)
-
-    def send_all(source, target, which, at):
-        def one(i, carry):
-            to = peer(N - 1 - i)
-            pltpu.make_async_remote_copy(
-                src_ref=source.at[at(to)],
-                dst_ref=target.at[me],
-                send_sem=sems.at[which],
-                recv_sem=rems.at[which],
-                device_id={"ctx": to},
-                device_id_type=MESH,
-            ).start()
-            return carry
-
-        lax.fori_loop(0, N - 1, one, 0, unroll=7)
+    for to in peers:
+        pl.semaphore_signal(barrier, inc=1, device_id={"ctx": to}, device_id_type=MESH)
+
+    operands = (
+        (st_any, st_ref), (rate_any, rate_ref), (x_any, x_ref), (b_any, b_ref),
+        (g_any, g_ref), (c_any, c_ref),
+    )
+    copies = [
+        pltpu.make_async_copy(there, here, loads.at[k]) for k, (there, here) in enumerate(operands)
+    ]
+    for copy in copies:
+        copy.start()
+
+    def send(source, target, which, to):
+        pltpu.make_async_remote_copy(
+            src_ref=source,
+            dst_ref=target,
+            send_sem=sems.at[which],
+            recv_sem=rems.at[which],
+            device_id={"ctx": to},
+            device_id_type=MESH,
+        ).start()
+
+    def send_all(source, target, which):
+        for to in peers:
+            send(source.at[to], target.at[me], which, to)
 
     def wait_all(sem, which, like):
-        some = like.at[pl.ds(0, N - 1)]
+        some = like.at[pl.ds(0, like.shape[0] - 1)]
         pltpu.make_async_copy(some, some, sem.at[which]).wait()
 
+    copies[0].wait()
+    copies[1].wait()
     head = iota((H, T), 0)
     rate = jnp.zeros((H, T), F32)
     for h in range(H):
@@ -118,6 +130,8 @@
             buffer[2 * k] = jnp.where(low_half, one, pltpu.roll(two, 4, 0))
             buffer[2 * k + 1] = jnp.where(low_half, pltpu.roll(one, 4, 0), two)
 
+    copies[2].wait()
+    copies[3].wait()
     for i in range(2):
         x, b = x_ref[0, i], b_ref[0, i]
         xs.append(split(x))
@@ -128,9 +142,12 @@
     recv_s[me] = send_s[me]
 
     pl.semaphore_wait(barrier, N - 1)
-    send_all(dec, decs, 0, lambda to: to // 8)
-    send_all(send_s, recv_s, 1, lambda to: to)
-
+    for to in peers:
+        send(dec.at[to // 8], decs.at[me], 0, to)
+    send_all(send_s, recv_s, 1)
+
+    copies[4].wait()
+    copies[5].wait()
     for i in range(2):
         g, c = g_ref[0, i], c_ref[0, i]
         gs.append(split(g))
@@ -139,7 +156,7 @@
     adjoint = [mm(gw[i], cs[i], TN) for i in range(2)]
     pack(adjoint[0], adjoint[1], send_a)
     recv_a[me] = send_a[me]
-    send_all(send_a, recv_a, 2, lambda to: to)
+    send_all(send_a, recv_a, 2)
 
     lane_head = iota((T, W), 1) // PW
     t_wide, s_wide = iota((T, H * T), 0), iota((T, H * T), 1) % T
@@ -212,11 +229,11 @@
     wait_all(rems, 1, recv_s)
     scan(recv_s, out_s, True)
     in_s[me] = out_s[me]
-    send_all(out_s, in_s, 3, lambda to: to)
+    send_all(out_s, in_s, 3)
     wait_all(rems, 2, recv_a)
     scan(recv_a, out_a, False)
     in_a[me] = out_a[me]
-    send_all(out_a, in_a, 4, lambda to: to)
+    send_all(out_a, in_a, 4)
 
     d_cum[1] = within(1)
 
@@ -259,29 +276,52 @@
     wait_all(sems, 4, out_a)
 
 
+def leave(*refs):
+    n = len(refs) // 2
+    copies = [
+        pltpu.make_async_copy(here, there, refs[-1].at[k])
+        for k, (here, there) in enumerate(zip(refs[:n], refs[n : 2 * n]))
+    ]
+    for copy in copies:
+        copy.start()
+    for copy in copies:
+        copy.wait()
+
+
 def per_device(inputs, b_matrix, c_matrix, step_sizes, decay_rate, cotangent):
     vmem = pl.BlockSpec(memory_space=pltpu.VMEM)
-    smem = pl.BlockSpec(memory_space=pltpu.SMEM)
+    hbm = pl.BlockSpec(memory_space=pltpu.HBM)
     chunks = pltpu.VMEM((N, 8, S), F32)
-    return pl.pallas_call(
+    outs = [jax.ShapeDtypeStruct(a.shape, F32) for a in (inputs, b_matrix, c_matrix, step_sizes)]
+    results = pl.pallas_call(
         kernel,
         name="mirrored_scan",
-        out_shape=[
-            jax.ShapeDtypeStruct(a.shape, F32) for a in (inputs, b_matrix, c_matrix, step_sizes)
-        ],
-        in_specs=[vmem, vmem, vmem, vmem, smem, vmem],
+        out_shape=outs,
+        in_specs=[hbm] * 6,
         out_specs=[vmem] * 4,
         scratch_shapes=[
+            *[pltpu.VMEM(a.shape, F32) for a in (inputs, b_matrix, c_matrix, step_sizes)],
+            pltpu.SMEM(decay_rate.shape, F32),
+            pltpu.VMEM(cotangent.shape, F32),
             pltpu.VMEM((H, 2, S), F32),
             pltpu.VMEM((N, 2, S), F32),
             *[chunks] * 9,
             pltpu.SemaphoreType.DMA((5,)),
             pltpu.SemaphoreType.DMA((5,)),
+            pltpu.SemaphoreType.DMA((6,)),
         ],
         compiler_params=pltpu.CompilerParams(
-            collective_id=0, has_side_effects=True, vmem_limit_bytes=40 << 20
+            collective_id=0, has_side_effects=True, vmem_limit_bytes=60 << 20
         ),
     )(inputs, b_matrix, c_matrix, step_sizes, decay_rate, cotangent)
+    return pl.pallas_call(
+        leave,
+        name="leave",
+        out_shape=results,
+        in_specs=[vmem] * 4,
+        out_specs=[hbm] * 4,
+        scratch_shapes=[pltpu.SemaphoreType.DMA((4,))],
+    )(*results)
 
 
 def solution(mesh):

time: 59.1 us -> 50.5 us (0.85)
  local copies, waits for them, and re-layouts: 7.34 us -> 0 us
  Pallas kernels: 50.8 us -> 49 us
    unnamed x16 -> x0, local copies, waits for them, and re-layouts: 7.34 us -> none
    pallas_call x1 -> x2, Pallas kernels: 50.8 us -> 49 us  [the longest x1 47.3 us: per_device(): pl.pallas_call(kernel, name='mirrored_scan', out_shape=outs, in_specs=[hb...]
where the time goes in v2:
time: 50.5 us; the launch traced here: 49.6 us
  Pallas kernels  49 us (97%)
  between operations  0.64 us (1%)
    pallas_call x1, Pallas kernels, per_device(): pl.pallas_call(kernel, name='mirrored_scan', out_shape=outs, in_specs=[hb...  47.3 us
    pallas_call x1, Pallas kernels, per_device(): pl.pallas_call(leave, name='leave', out_shape=results, in_specs=[vmem] *...  1.68 us

profile of v2, /device:TPU:1, one launch (start us, length us, event | category | flops | bytes accessed | tf_op | source)
XLA Modules:
  0.0 49.6 jit_solution(13845992361404752558)
XLA Ops:
  0.6 47.3 %mirrored_scan.1 = (f32[1,2,64,256]{3,2,1,0:T(8,128)}, f32[1,2,64,128]{3,2,1,0:T(8,128)}, f32[1,2,64,128]{3,2,1,0:T(8,128)}, f32[1,2,8,64]{3,2,1,0:T(8,128)}) custom-call(f32[1,2,64,256]{3,2,1,0:T(8,128)} %x_any.1, f32[1,2,64,128]{3,2,1,0:T(8,128)} %b_any.1, f32[1,2,64,128]{3,2,1,0:T(8,128)} %c_any.1, f32[1,2,8,64]{3,2,1,0:T(8,128)} %st_any.1, f32[8]{0:T(128)} %rate_any.1, ...), custom_call_target="tpu_custom_call" | custom-call | tf_op jit(solution)/shard_map/mirrored_scan/pallas_call | solution.py:296
  47.9 1.7 %leave.1 = (f32[1,2,64,256]{3,2,1,0:T(8,128)}, f32[1,2,64,128]{3,2,1,0:T(8,128)}, f32[1,2,64,128]{3,2,1,0:T(8,128)}, f32[1,2,8,64]{3,2,1,0:T(8,128)}) custom-call(f32[1,2,64,256]{3,2,1,0:T(8,128)} %get-tuple-element.8.refs_0_, f32[1,2,64,128]{3,2,1,0:T(8,128)} %get-tuple-element.9.refs_1_, f32[1,2,64,128]{3,2,1,0:T(8,128)} %get-tuple-element.10.refs_2_, ...), custom_call_target="tpu_custom_call" | custom-call | tf_op jit(solution)/shard_map/leave/pallas_call | solution.py:317

commit v3 on v2

--- a/solution.py
+++ b/solution.py
@@ -12,7 +12,8 @@
 HIGHEST = lax.Precision.HIGHEST
 MESH = pl.DeviceIdType.MESH
 
-N = 64
+N = 32
+X, Z = 4, 8
 T = 64
 H = 8
 PW = 32
@@ -50,24 +51,23 @@
     x_any, b_any, c_any, st_any, rate_any, g_any,
     gx_ref, gb_ref, gc_ref, gs_ref,
     x_ref, b_ref, c_ref, st_ref, rate_ref, g_ref,
-    dec, decs, tiles, send_s, send_a, recv_s, recv_a, out_s, out_a, in_s, in_a,
+    dec, decs, before_z, after_z, across, across_y,
+    send_s, send_a, recv_s, recv_a, sum_s, sum_a, sum_sy, sum_ay, out_s, out_a, in_s, in_a,
     sems, rems, loads,
 ):
     me = lax.axis_index("ctx")
     px, py, pz = me // 16, (me // 8) % 2, me % 8
-    x_part = [lax.rem(px + k, 4) * 16 for k in range(4)]
-    y_part = [lax.rem(py + k, 2) * 8 for k in range(2)]
-    z_part = [lax.rem(pz + k, 8) for k in range(8)]
-    peers = [
-        x_part[x] + y_part[y] + z_part[z]
-        for z in (4, 3, 5, 2, 6, 1, 7, 0)
-        for y in (1, 0)
-        for x in (2, 1, 3, 0)
-    ][:-1]
+    mine = px * Z + pz
+    x_at = [lax.rem(px + k, X) for k in range(X)]
+    z_at = [lax.rem(pz + k, Z) for k in range(Z)]
+    partner = px * 16 + (1 - py) * 8 + pz
+    far_x, far_z = (2, 1, 3, 0), (4, 3, 5, 2, 6, 1, 7, 0)
+    by_x = [(x_at[x] * 16 + py * 8 + z_at[z], x_at[x] * Z + z_at[z]) for x in far_x for z in far_z]
+    by_z = [(x_at[x] * 16 + py * 8 + z_at[z], x_at[x] * Z + z_at[z]) for z in far_z for x in far_x]
+    by_x, by_z = by_x[:-1], by_z[:-1]
 
     barrier = pltpu.get_barrier_semaphore()
-
-    for to in peers:
+    for to in [partner] + [to for to, _ in by_x]:
         pl.semaphore_signal(barrier, inc=1, device_id={"ctx": to}, device_id_type=MESH)
 
     operands = (
@@ -90,13 +90,15 @@
             device_id_type=MESH,
         ).start()
 
-    def send_all(source, target, which):
-        for to in peers:
-            send(source.at[to], target.at[me], which, to)
+    def send_all(source, target, which, peers):
+        for to, place in peers:
+            send(source.at[place], target.at[mine], which, to)
+
+    def wait(sem, which, some):
+        pltpu.make_async_copy(some, some, sem.at[which]).wait()
 
     def wait_all(sem, which, like):
-        some = like.at[pl.ds(0, like.shape[0] - 1)]
-        pltpu.make_async_copy(some, some, sem.at[which]).wait()
+        wait(sem, which, like.at[pl.ds(0, N - 1)])
 
     copies[0].wait()
     copies[1].wait()
@@ -107,7 +109,7 @@
     row_t, col_t = iota((T, T), 0), iota((T, T), 1)
     tri = (col_t <= row_t).astype(F32)
     sel32 = (iota((H, W), 1) // PW == iota((H, W), 0)).astype(F32)
-    cum, spread, from_start, to_end = [], [], [], []
+    cum, from_start, to_end = [], [], []
     for i in range(2):
         logd = -rate * st_ref[0, i]
         total = jnp.exp(jnp.sum(logd, axis=1, keepdims=True))
@@ -116,20 +118,11 @@
         cum_i = exact(tri, logd, NT)
         wide = exact(cum_i, sel32)
         cum.append(cum_i)
-        spread.append(wide)
         from_start.append(jnp.exp(wide))
         to_end.append(jnp.exp(wide[T - 1 : T] - wide))
-    decs[me] = dec[me // 8]
-
-    low_half = iota((8, S), 0) < 4
+    decs[mine] = dec[mine // 4]
+
     xw, gw, bs, cs, xs, gs = [], [], [], [], [], []
-
-    def pack(first, second, buffer):
-        for k in range(N // 2):
-            one, two = first[8 * k : 8 * k + 8], second[8 * k : 8 * k + 8]
-            buffer[2 * k] = jnp.where(low_half, one, pltpu.roll(two, 4, 0))
-            buffer[2 * k + 1] = jnp.where(low_half, pltpu.roll(one, 4, 0), two)
-
     copies[2].wait()
     copies[3].wait()
     for i in range(2):
@@ -137,14 +130,13 @@
         xs.append(split(x))
         bs.append(split(b))
         xw.append(split(x * to_end[i]))
-    state = [mm(xw[i], bs[i], TN) for i in range(2)]
-    pack(state[0], state[1], send_s)
-    recv_s[me] = send_s[me]
-
-    pl.semaphore_wait(barrier, N - 1)
-    for to in peers:
-        send(dec.at[to // 8], decs.at[me], 0, to)
-    send_all(send_s, recv_s, 1)
+        send_s[:, 8 * i : 8 * i + 8, :] = mm(xw[i], bs[i], TN).reshape(N, 8, S)
+    recv_s[mine] = send_s[mine]
+
+    pl.semaphore_wait(barrier, N)
+    for to, place in by_x:
+        send(dec.at[place // 4], decs.at[mine], 0, to)
+    send_all(send_s, recv_s, 1, by_x)
 
     copies[4].wait()
     copies[5].wait()
@@ -153,10 +145,9 @@
         gs.append(split(g))
         cs.append(split(c))
         gw.append(split(g * from_start[i]))
-    adjoint = [mm(gw[i], cs[i], TN) for i in range(2)]
-    pack(adjoint[0], adjoint[1], send_a)
-    recv_a[me] = send_a[me]
-    send_all(send_a, recv_a, 2)
+        send_a[:, 8 * i : 8 * i + 8, :] = mm(gw[i], cs[i], TN).reshape(N, 8, S)
+    recv_a[mine] = send_a[mine]
+    send_all(send_a, recv_a, 2, by_x)
 
     lane_head = iota((T, W), 1) // PW
     t_wide, s_wide = iota((T, H * T), 0), iota((T, H * T), 1) % T
@@ -203,56 +194,96 @@
 
     d_cum = [within(0), None]
 
-    def scan(received, result, low_first):
-        keep = low_half if low_first else jnp.logical_not(low_half)
-
-        def up(j, carry):
-            result[j] = carry
-            return tiles[j] * carry + received[j]
-
-        top = lax.fori_loop(0, N, up, jnp.zeros((8, S), F32), unroll=8)
-
-        def down(i, carry):
-            j = N - 1 - i
-            result[j] = jnp.where(keep, result[j], carry)
-            return tiles[j] * carry + received[j]
-
-        lax.fori_loop(0, N, down, pltpu.roll(top, 4, 0), unroll=8)
-
     wait_all(rems, 0, decs)
-
-    def spread_decay(j, carry):
-        tiles[j] = jnp.where(low_half, decs[j, 0:1, :], decs[j, 1:2, :])
-        return carry
-
-    lax.fori_loop(0, N, spread_decay, 0, unroll=8)
+    for x in range(X):
+        one = jnp.ones((2, S), F32)
+        for z in range(Z):
+            before_z[x * Z + z] = one
+            one *= decs[x * Z + z]
+        across[x] = one
+        one = jnp.ones((2, S), F32)
+        for z in reversed(range(Z)):
+            after_z[x * Z + z] = one
+            one *= decs[x * Z + z]
+    send(across, across_y, 3, partner)
+
+    def rows(slot):
+        return pl.ds(8 * slot, 8)
+
+    def scan(received, result, sums, first):
+        for slot, order in ((first, range(Z)), (1 - first, range(Z - 1, -1, -1))):
+            carry = [jnp.zeros((8, S), F32)] * X
+            for z in order:
+                for x in range(X):
+                    at = x * Z + z
+                    result[at, rows(slot), :] = carry[x]
+                    carry[x] = (
+                        decs[at, slot : slot + 1, :] * carry[x] + received[at, rows(slot), :]
+                    )
+            for x in range(X):
+                sums[x, rows(slot), :] = carry[x]
+
+    def compose(result, sums, sums_y, first):
+        is_low = py == 0
+
+        def planes(ours, theirs, slot):
+            pairs = [(ours(x, slot), theirs(x, slot)) for x in range(X)]
+            return [
+                jnp.where(is_low == (y == 0), a, b) for a, b in pairs for y in range(2)
+            ]
+
+        def decay(ref):
+            return lambda x, slot: ref[x, slot : slot + 1, :]
+
+        def total(ref):
+            return lambda x, slot: ref[x, rows(slot), :]
+
+        carry = jnp.zeros((8, S), F32)
+        for slot, order, along in (
+            (first, range(2 * X), before_z),
+            (1 - first, range(2 * X - 1, -1, -1), after_z),
+        ):
+            decays = planes(decay(across), decay(across_y), slot)
+            totals = planes(total(sums), total(sums_y), slot)
+            entering = [None] * (2 * X)
+            for p in order:
+                entering[p] = carry
+                carry = decays[p] * carry + totals[p]
+            for x in range(X):
+                plane = jnp.where(is_low, entering[2 * x], entering[2 * x + 1])
+                for z in range(Z):
+                    at = x * Z + z
+                    result[at, rows(slot), :] += along[at, slot : slot + 1, :] * plane
+
     wait_all(rems, 1, recv_s)
-    scan(recv_s, out_s, True)
-    in_s[me] = out_s[me]
-    send_all(out_s, in_s, 3)
+    scan(recv_s, out_s, sum_s, 0)
+    send(sum_s, sum_sy, 4, partner)
     wait_all(rems, 2, recv_a)
-    scan(recv_a, out_a, False)
-    in_a[me] = out_a[me]
-    send_all(out_a, in_a, 4)
+    scan(recv_a, out_a, sum_a, 1)
+    send(sum_a, sum_ay, 5, partner)
+    wait(rems, 3, across_y)
+    wait(rems, 4, sum_sy)
+    compose(out_s, sum_s, sum_sy, 0)
+    in_s[mine] = out_s[mine]
+    send_all(out_s, in_s, 6, by_z)
+    wait(rems, 5, sum_ay)
+    compose(out_a, sum_a, sum_ay, 1)
+    in_a[mine] = out_a[mine]
+    send_all(out_a, in_a, 7, by_z)
 
     d_cum[1] = within(1)
 
     def unpack(buffer):
-        first, second = [], []
-        for k in range(N // 2):
-            one, two = buffer[2 * k], buffer[2 * k + 1]
-            first.append(jnp.where(low_half, one, pltpu.roll(two, 4, 0)))
-            second.append(jnp.where(low_half, pltpu.roll(one, 4, 0), two))
-        return jnp.concatenate(first, axis=0), jnp.concatenate(second, axis=0)
-
-    wait_all(rems, 3, in_s)
+        return [buffer[:, 8 * i : 8 * i + 8, :].reshape(W, S) for i in range(2)]
+
+    wait_all(rems, 6, in_s)
     entering = unpack(in_s)
     for i in range(2):
         parts = split(entering[i])
         carried = mm(cs[i], parts, NT)
         gc_ref[0, i] += mm(gw[i], parts)
         d_cum[i] += by_head(g_ref[0, i] * from_start[i] * carried, pick32)
-    wait_all(rems, 4, in_a)
+    wait_all(rems, 7, in_a)
     leaving = unpack(in_a)
     after = (row_t >= col_t).astype(F32)
     before = (row_t < col_t).astype(F32)
@@ -272,8 +303,11 @@
     wait_all(sems, 0, decs)
     wait_all(sems, 1, send_s)
     wait_all(sems, 2, send_a)
-    wait_all(sems, 3, out_s)
-    wait_all(sems, 4, out_a)
+    wait(sems, 3, across)
+    wait(sems, 4, sum_s)
+    wait(sems, 5, sum_a)
+    wait_all(sems, 6, out_s)
+    wait_all(sems, 7, out_a)
 
 
 def leave(*refs):
@@ -291,7 +325,8 @@
 def per_device(inputs, b_matrix, c_matrix, step_sizes, decay_rate, cotangent):
     vmem = pl.BlockSpec(memory_space=pltpu.VMEM)
     hbm = pl.BlockSpec(memory_space=pltpu.HBM)
-    chunks = pltpu.VMEM((N, 8, S), F32)
+    chunks = pltpu.VMEM((N, 16, S), F32)
+    sums = pltpu.VMEM((X, 16, S), F32)
     outs = [jax.ShapeDtypeStruct(a.shape, F32) for a in (inputs, b_matrix, c_matrix, step_sizes)]
     results = pl.pallas_call(
         kernel,
@@ -304,10 +339,13 @@
             pltpu.SMEM(decay_rate.shape, F32),
             pltpu.VMEM(cotangent.shape, F32),
             pltpu.VMEM((H, 2, S), F32),
-            pltpu.VMEM((N, 2, S), F32),
-            *[chunks] * 9,
-            pltpu.SemaphoreType.DMA((5,)),
-            pltpu.SemaphoreType.DMA((5,)),
+            *[pltpu.VMEM((N, 2, S), F32)] * 3,
+            *[pltpu.VMEM((X, 2, S), F32)] * 2,
+            *[chunks] * 4,
+            *[sums] * 4,
+            *[chunks] * 4,
+            pltpu.SemaphoreType.DMA((8,)),
+            pltpu.SemaphoreType.DMA((8,)),
             pltpu.SemaphoreType.DMA((6,)),
         ],
         compiler_params=pltpu.CompilerParams(
@@ -317,7 +355,7 @@
     return pl.pallas_call(
         leave,
         name="leave",
-        out_shape=results,
+        out_shape=outs,
         in_specs=[vmem] * 4,
         out_specs=[hbm] * 4,
         scratch_shapes=[pltpu.SemaphoreType.DMA((4,))],

time: 50.5 us -> 47.9 us (0.949)
  the two profiles are of different devices: /device:TPU:1 before, /device:TPU:2 now
where the time goes in v3:
time: 47.9 us; the launch traced here: 47.7 us
  Pallas kernels  47.1 us (98%)
  between operations  0.64 us (1%)
    pallas_call x1, Pallas kernels, per_device(): pl.pallas_call(kernel, name='mirrored_scan', out_shape=outs, in_specs=[hb...  45.4 us
    pallas_call x1, Pallas kernels, per_device(): pl.pallas_call(leave, name='leave', out_shape=outs, in_specs=[vmem] * 4,...  1.68 us

profile of v3, /device:TPU:2, one launch (start us, length us, event | category | flops | bytes accessed | tf_op | source)
XLA Modules:
  0.0 47.7 jit_solution(13604845719360351256)
XLA Ops:
  0.6 45.4 %mirrored_scan.1 = (f32[1,2,64,256]{3,2,1,0:T(8,128)}, f32[1,2,64,128]{3,2,1,0:T(8,128)}, f32[1,2,64,128]{3,2,1,0:T(8,128)}, f32[1,2,8,64]{3,2,1,0:T(8,128)}) custom-call(f32[1,2,64,256]{3,2,1,0:T(8,128)} %x_any.1, f32[1,2,64,128]{3,2,1,0:T(8,128)} %b_any.1, f32[1,2,64,128]{3,2,1,0:T(8,128)} %c_any.1, f32[1,2,8,64]{3,2,1,0:T(8,128)} %st_any.1, f32[8]{0:T(128)} %rate_any.1, ...), custom_call_target="tpu_custom_call" | custom-call | tf_op jit(solution)/shard_map/mirrored_scan/pallas_call | solution.py:331
  46.0 1.7 %leave.1 = (f32[1,2,64,256]{3,2,1,0:T(8,128)}, f32[1,2,64,128]{3,2,1,0:T(8,128)}, f32[1,2,64,128]{3,2,1,0:T(8,128)}, f32[1,2,8,64]{3,2,1,0:T(8,128)}) custom-call(f32[1,2,64,256]{3,2,1,0:T(8,128)} %get-tuple-element.8.refs_0_, f32[1,2,64,128]{3,2,1,0:T(8,128)} %get-tuple-element.9.refs_1_, f32[1,2,64,128]{3,2,1,0:T(8,128)} %get-tuple-element.10.refs_2_, ...), custom_call_target="tpu_custom_call" | custom-call | tf_op jit(solution)/shard_map/leave/pallas_call | solution.py:355

commit v4 on v2

v4 whole, which is shorter than its diff:
```python
import functools

import jax
import jax.numpy as jnp
from jax import lax
from jax.experimental import pallas as pl
from jax.experimental.pallas import tpu as pltpu
from jax.sharding import PartitionSpec as P

F32 = jnp.float32
BF16 = jnp.bfloat16
HIGHEST = lax.Precision.HIGHEST
MESH = pl.DeviceIdType.MESH

Z = 8
X, Y = 4, 2
PIECES = 4
PART = 16
T = 64
H = 8
PW = 32
W = H * PW
S = 128

NN = (((1,), (0,)), ((), ()))
NT = (((1,), (1,)), ((), ()))
TN = (((0,), (0,)), ((), ()))


def split(a):
    high = a.astype(BF16)
    low = (a - high.astype(F32)).astype(BF16)
    return high, low


def dot(a, b, dims=NN):
    return lax.dot_general(a, b, dims, preferred_element_type=F32)


def mm(a, b, dims=NN):
    return dot(a[0], b[0], dims) + (dot(a[0], b[1], dims) + dot(a[1], b[0], dims))


def rows_mm(a, b, dims=NN):
    n = a[0].shape[0]
    both = dot(jnp.concatenate(a, axis=0), b[0], dims)
    return both[:n] + (both[n:] + dot(a[0], b[1], dims))


def exact(a, b, dims=NN):
    return lax.dot_general(a, b, dims, precision=HIGHEST, preferred_element_type=F32)


def iota(shape, dim):
    return lax.broadcasted_iota(jnp.int32, shape, dim)


def kernel(
    x_any, b_any, c_any, st_any, rate_any, g_any,
    gx_ref, gb_ref, gc_ref, gs_ref,
    x_ref, b_ref, c_ref, st_ref, rate_ref, g_ref,
    dec, decs, before_z, after_z, line_decs, outgoing, arrived, line_sums, result, returned,
    sems, rems, loads,
):
    me = lax.axis_index("ctx")
    line, pz = me // Z, me % Z
    px, py = line // Y, line % Y
    z_at = [lax.rem(pz + k, Z) for k in (4, 3, 5, 2, 6, 1, 7)]
    lines = [
        lax.rem(px + x, X) * Y + lax.rem(py + y, Y) for y in (1, 0) for x in (2, 1, 3, 0)
    ][:-1]

    barrier = pltpu.get_barrier_semaphore()
    for to in [other * Z + pz for other in lines] + [line * Z + z for z in z_at]:
        pl.semaphore_signal(barrier, inc=1, device_id={"ctx": to}, device_id_type=MESH)

    operands = (
        (st_any, st_ref), (rate_any, rate_ref), (x_any, x_ref), (b_any, b_ref),
        (g_any, g_ref), (c_any, c_ref),
    )
    copies = [
        pltpu.make_async_copy(there, here, loads.at[k]) for k, (there, here) in enumerate(operands)
    ]
    for copy in copies:
        copy.start()

    def send(source, target, which, to):
        pltpu.make_async_remote_copy(
            src_ref=source,
            dst_ref=target,
            send_sem=sems.at[which],
            recv_sem=rems.at[which],
            device_id={"ctx": to},
            device_id_type=MESH,
        ).start()

    def wait(sem, which, like):
        some = like.at[pl.ds(0, 7)]
        pltpu.make_async_copy(some, some, sem.at[which]).wait()

    TO_OWNER, TO_LINES, BACK = 2, 2 + PIECES, 2 + 2 * PIECES

    copies[0].wait()
    copies[1].wait()
    head = iota((H, T), 0)
    rate = jnp.zeros((H, T), F32)
    for h in range(H):
        rate = jnp.where(head == h, rate_ref[h], rate)
    row_t, col_t = iota((T, T), 0), iota((T, T), 1)
    tri = (col_t <= row_t).astype(F32)
    sel32 = (iota((H, W), 1) // PW == iota((H, W), 0)).astype(F32)
    cum, from_start, to_end = [], [], []
    for i in range(2):
        logd = -rate * st_ref[0, i]
        total = jnp.exp(jnp.sum(logd, axis=1, keepdims=True))
        for h in range(H):
            dec[h, pl.ds(i, 1), :] = jnp.broadcast_to(total[h : h + 1], (1, S))
        cum_i = exact(tri, logd, NT)
        wide = exact(cum_i, sel32)
        cum.append(cum_i)
        from_start.append(jnp.exp(wide))
        to_end.append(jnp.exp(wide[T - 1 : T] - wide))
    decs[pz] = dec[pz]

    xw, gw, bs, cs, xs, gs = [], [], [], [], [], []

    def slot_rows(i):
        return slice(PART * i, PART * i + PART)

    def pack(state, i, first_piece):
        heads = state.reshape(H, PW, S)
        for part in range(2):
            outgoing[first_piece + part, :, slot_rows(i), :] = heads[:, slot_rows(part)]

    def to_owners(k):
        arrived[k, pz] = outgoing[k, pz]
        for z in z_at:
            send(outgoing.at[k, z], arrived.at[k, pz], TO_OWNER + k, line * Z + z)

    copies[2].wait()
    copies[3].wait()
    for i in range(2):
        x, b = x_ref[0, i], b_ref[0, i]
        xs.append(split(x))
        bs.append(split(b))
        xw.append(split(x * to_end[i]))
        pack(mm(xw[i], bs[i], TN), i, 0)

    pl.semaphore_wait(barrier, 14)
    for z in z_at:
        send(dec.at[z], decs.at[pz], 0, line * Z + z)
    to_owners(0)
    to_owners(1)

    copies[4].wait()
    copies[5].wait()
    for i in range(2):
        g, c = g_ref[0, i], c_ref[0, i]
        gs.append(split(g))
        cs.append(split(c))
        gw.append(split(g * from_start[i]))
        pack(mm(gw[i], cs[i], TN), i, 2)
    to_owners(2)

    lane_head = iota((T, W), 1) // PW
    t_wide, s_wide = iota((T, H * T), 0), iota((T, H * T), 1) % T
    sel64 = (iota((H, H * T), 1) // T == iota((H, H * T), 0)).astype(F32)
    pick = (iota((H * T, H), 0) // T == iota((H * T, H), 1)).astype(BF16)
    pick32 = (iota((W, H), 0) // PW == iota((W, H), 1)).astype(BF16)
    zero = jnp.zeros((), BF16)

    def stacked(parts):
        return [
            jnp.concatenate([jnp.where(lane_head == h, part, zero) for h in range(H)], axis=0)
            for part in parts
        ]

    def twice(parts):
        return [jnp.concatenate([part, part], axis=0) for part in parts]

    def folded(a):
        return a[:, :128] + a[:, 128:256] + (a[:, 256:384] + a[:, 384:])

    def by_head(a, selection):
        high, low = split(a)
        return dot(high, selection) + dot(low, selection)

    def within(i):
        columns = exact(cum[i], sel64)
        row = jnp.sum(jnp.where(t_wide == s_wide, columns, 0.0), axis=0, keepdims=True)
        gap = columns - row
        forward = jnp.exp(jnp.where(s_wide <= t_wide, gap, -1e30))
        backward = jnp.exp(jnp.where(s_wide >= t_wide, -gap, -1e30))
        b_twice, c_twice = twice(bs[i]), twice(cs[i])
        x_stack, g_stack = stacked(xs[i]), stacked(gs[i])
        scores = jnp.concatenate([mm(cs[i], b_twice, NT)] * 4, axis=1)
        scores_back = jnp.concatenate([mm(bs[i], c_twice, NT)] * 4, axis=1)
        inner = forward * mm(gs[i], x_stack, NT)
        inner_back = backward * mm(xs[i], g_stack, NT)
        gc_ref[0, i] = mm(split(folded(inner)), b_twice)
        gb_ref[0, i] = mm(split(folded(inner_back)), c_twice)
        gx_ref[0, i] = mm(split(scores_back * backward), g_stack)
        off = s_wide != t_wide
        return by_head(jnp.where(off, scores * inner, 0.0), pick) - by_head(
            jnp.where(off, scores_back * inner_back, 0.0), pick
        )

    def scan(k):
        first = k // 2
        for slot, order in ((first, range(Z)), (1 - first, range(Z - 1, -1, -1))):
            carry = jnp.zeros((PART, S), F32)
            for z in order:
                result[k, z, slot_rows(slot), :] = carry
                carry = decs[z, slot : slot + 1, :] * carry + arrived[k, z, slot_rows(slot), :]
            line_sums[k, line, slot_rows(slot), :] = carry

    def compose(k):
        first = k // 2
        carry = jnp.zeros((PART, S), F32)
        for slot, order, along_z in (
            (first, range(Z), before_z),
            (1 - first, range(Z - 1, -1, -1), after_z),
        ):
            enters = jnp.zeros((PART, S), F32)
            for p in order:
                enters = jnp.where(line == p, carry, enters)
                carry = (
                    line_decs[p, slot : slot + 1, :] * carry + line_sums[k, p, slot_rows(slot), :]
                )
            for z in range(Z):
                result[k, z, slot_rows(slot), :] += along_z[z, slot : slot + 1, :] * enters

    def to_lines(k):
        wait(rems, TO_OWNER + k, arrived.at[k])
        scan(k)
        for other in lines:
            send(
                line_sums.at[k, line], line_sums.at[k, line], TO_LINES + k, other * Z + pz
            )

    def back(k):
        wait(rems, TO_LINES + k, line_sums.at[k])
        compose(k)
        returned[k, pz] = result[k, pz]

        def to(z):
            send(result.at[k, z], returned.at[k, pz], BACK + k, line * Z + z)

        pl.when(pz != 0)(lambda: to(0))
        for z in z_at:
            pl.when(z != 0)(functools.partial(to, z))

    d_cum = [within(0), None]

    wait(rems, 0, decs)
    one = jnp.ones((2, S), F32)
    for z in range(Z):
        before_z[z] = one
        one *= decs[z]
    line_decs[line] = one
    one = jnp.ones((2, S), F32)
    for z in reversed(range(Z)):
        after_z[z] = one
        one *= decs[z]
    for other in lines:
        send(line_decs.at[line], line_decs.at[line], 1, other * Z + pz)

    to_lines(0)
    to_owners(3)
    to_lines(1)
    to_lines(2)
    wait(rems, 1, line_decs)
    back(0)
    to_lines(3)
    back(1)
    back(2)
    back(3)

    d_cum[1] = within(1)

    def unpack(first_piece):
        for part in range(2):
            wait(rems, BACK + first_piece + part, returned.at[first_piece + part])
        return [
            jnp.concatenate(
                [returned[first_piece + part, :, slot_rows(i), :] for part in range(2)], axis=1
            ).reshape(W, S)
            for i in range(2)
        ]

    after = (row_t >= col_t).astype(F32)
    before = (row_t < col_t).astype(BF16)

    def along(a, triangle):
        return sum(dot(part, triangle, TN) for part in split(a))

    entering = unpack(0)
    d_log = []
    for i in range(2):
        parts = split(entering[i])
        carried = rows_mm(cs[i], parts, NT)
        gc_ref[0, i] += rows_mm(gw[i], parts)
        d_cum[i] += by_head(g_ref[0, i] * from_start[i] * carried, pick32)
        d_log.append(exact(d_cum[i], after, TN))
    ends = [
        jnp.concatenate([dec[h, pl.ds(i, 1), 0:1] for h in range(H)], axis=0) for i in range(2)
    ]
    leaving = unpack(2)
    for i in range(2):
        parts = split(leaving[i])
        weighted = to_end[i] * rows_mm(bs[i], parts, NT)
        gx_ref[0, i] += weighted
        gb_ref[0, i] += rows_mm(xw[i], parts)
        fresh = by_head(x_ref[0, i] * weighted, pick32)
        product = jnp.sum((leaving[i] * entering[i]).reshape(H, PW, S), axis=1)
        through = jnp.sum(product, axis=1, keepdims=True) * ends[i]
        gs_ref[0, i] = -rate * (d_log[i] + along(fresh, before) + through)

    wait(sems, 0, decs)
    wait(sems, 1, line_decs)
    for k in range(PIECES):
        wait(sems, TO_OWNER + k, outgoing.at[k])
        wait(sems, TO_LINES + k, line_sums.at[k])
        wait(sems, BACK + k, result.at[k])


def leave(*refs):
    n = len(refs) // 2
    copies = [
        pltpu.make_async_copy(here, there, refs[-1].at[k])
        for k, (here, there) in enumerate(zip(refs[:n], refs[n : 2 * n]))
    ]
    for copy in copies:
        copy.start()
    for copy in copies:
        copy.wait()


def per_device(inputs, b_matrix, c_matrix, step_sizes, decay_rate, cotangent):
    vmem = pl.BlockSpec(memory_space=pltpu.VMEM)
    hbm = pl.BlockSpec(memory_space=pltpu.HBM)
    decays = pltpu.VMEM((8, 2, S), F32)
    chunks = pltpu.VMEM((PIECES, 8, 2 * PART, S), F32)
    n_sems = 2 + 3 * PIECES
    outs = [jax.ShapeDtypeStruct(a.shape, F32) for a in (inputs, b_matrix, c_matrix, step_sizes)]
    results = pl.pallas_call(
        kernel,
        name="mirrored_scan",
        out_shape=outs,
        in_specs=[hbm] * 6,
        out_specs=[vmem] * 4,
        scratch_shapes=[
            *[pltpu.VMEM(a.shape, F32) for a in (inputs, b_matrix, c_matrix, step_sizes)],
            pltpu.SMEM(decay_rate.shape, F32),
            pltpu.VMEM(cotangent.shape, F32),
            *[decays] * 5,
            *[chunks] * 5,
            pltpu.SemaphoreType.DMA((n_sems,)),
            pltpu.SemaphoreType.DMA((n_sems,)),
            pltpu.SemaphoreType.DMA((6,)),
        ],
        compiler_params=pltpu.CompilerParams(
            collective_id=0, has_side_effects=True, vmem_limit_bytes=60 << 20
        ),
    )(inputs, b_matrix, c_matrix, step_sizes, decay_rate, cotangent)
    return pl.pallas_call(
        leave,
        name="leave",
        out_shape=outs,
        in_specs=[vmem] * 4,
        out_specs=[hbm] * 4,
        scratch_shapes=[pltpu.SemaphoreType.DMA((4,))],
    )(*results)


def solution(mesh):
    blocks = P("ctx", None, None, "tp")
    steps = P("ctx", None, "tp", None)
    return jax.shard_map(
        per_device,
        mesh=mesh,
        in_specs=(blocks, blocks, blocks, steps, P("tp"), blocks),
        out_specs=(blocks, blocks, blocks, steps),
        check_vma=False,
    )
```

time: 50.5 us -> 46 us (0.911)
  the two profiles are of different devices: /device:TPU:1 before, /device:TPU:8 now
where the time goes in v4:
time: 46 us; the launch traced here: 45.9 us
  Pallas kernels  45.2 us (98%)
  between operations  0.64 us (1%)
    pallas_call x1, Pallas kernels, per_device(): pl.pallas_call(kernel, name='mirrored_scan', out_shape=outs, in_specs=[hb...  43.6 us
    pallas_call x1, Pallas kernels, per_device(): pl.pallas_call(leave, name='leave', out_shape=outs, in_specs=[vmem] * 4,...  1.68 us

profile of v4, /device:TPU:8, one launch (start us, length us, event | category | flops | bytes accessed | tf_op | source)
XLA Modules:
  0.0 45.9 jit_solution(16622727153866569087)
XLA Ops:
  0.6 43.6 %mirrored_scan.1 = (f32[1,2,64,256]{3,2,1,0:T(8,128)}, f32[1,2,64,128]{3,2,1,0:T(8,128)}, f32[1,2,64,128]{3,2,1,0:T(8,128)}, f32[1,2,8,64]{3,2,1,0:T(8,128)}) custom-call(f32[1,2,64,256]{3,2,1,0:T(8,128)} %x_any.1, f32[1,2,64,128]{3,2,1,0:T(8,128)} %b_any.1, f32[1,2,64,128]{3,2,1,0:T(8,128)} %c_any.1, f32[1,2,8,64]{3,2,1,0:T(8,128)} %st_any.1, f32[8]{0:T(128)} %rate_any.1, ...), custom_call_target="tpu_custom_call" | custom-call | tf_op jit(solution)/shard_map/mirrored_scan/pallas_call | solution.py:346
  44.2 1.7 %leave.1 = (f32[1,2,64,256]{3,2,1,0:T(8,128)}, f32[1,2,64,128]{3,2,1,0:T(8,128)}, f32[1,2,64,128]{3,2,1,0:T(8,128)}, f32[1,2,8,64]{3,2,1,0:T(8,128)}) custom-call(f32[1,2,64,256]{3,2,1,0:T(8,128)} %get-tuple-element.8.refs_0_, f32[1,2,64,128]{3,2,1,0:T(8,128)} %get-tuple-element.9.refs_1_, f32[1,2,64,128]{3,2,1,0:T(8,128)} %get-tuple-element.10.refs_2_, ...), custom_call_target="tpu_custom_call" | custom-call | tf_op jit(solution)/shard_map/leave/pallas_call | solution.py:366

commit v5 on v4

--- a/solution.py
+++ b/solution.py
@@ -15,7 +15,7 @@
 Z = 8
 X, Y = 4, 2
 PIECES = 4
-PART = 16
+SLOTS = (0, 1, 1, 0)
 T = 64
 H = 8
 PW = 32
@@ -124,14 +124,6 @@
 
     xw, gw, bs, cs, xs, gs = [], [], [], [], [], []
 
-    def slot_rows(i):
-        return slice(PART * i, PART * i + PART)
-
-    def pack(state, i, first_piece):
-        heads = state.reshape(H, PW, S)
-        for part in range(2):
-            outgoing[first_piece + part, :, slot_rows(i), :] = heads[:, slot_rows(part)]
-
     def to_owners(k):
         arrived[k, pz] = outgoing[k, pz]
         for z in z_at:
@@ -144,7 +136,7 @@
         xs.append(split(x))
         bs.append(split(b))
         xw.append(split(x * to_end[i]))
-        pack(mm(xw[i], bs[i], TN), i, 0)
+        outgoing[i] = mm(xw[i], bs[i], TN).reshape(H, PW, S)
 
     pl.semaphore_wait(barrier, 14)
     for z in z_at:
@@ -159,7 +151,7 @@
         gs.append(split(g))
         cs.append(split(c))
         gw.append(split(g * from_start[i]))
-        pack(mm(gw[i], cs[i], TN), i, 2)
+        outgoing[3 - i] = mm(gw[i], cs[i], TN).reshape(H, PW, S)
     to_owners(2)
 
     lane_head = iota((T, W), 1) // PW
@@ -206,29 +198,23 @@
         )
 
     def scan(k):
-        first = k // 2
-        for slot, order in ((first, range(Z)), (1 - first, range(Z - 1, -1, -1))):
-            carry = jnp.zeros((PART, S), F32)
-            for z in order:
-                result[k, z, slot_rows(slot), :] = carry
-                carry = decs[z, slot : slot + 1, :] * carry + arrived[k, z, slot_rows(slot), :]
-            line_sums[k, line, slot_rows(slot), :] = carry
-
-    def compose(k):
-        first = k // 2
-        carry = jnp.zeros((PART, S), F32)
-        for slot, order, along_z in (
-            (first, range(Z), before_z),
-            (1 - first, range(Z - 1, -1, -1), after_z),
-        ):
-            enters = jnp.zeros((PART, S), F32)
-            for p in order:
-                enters = jnp.where(line == p, carry, enters)
-                carry = (
-                    line_decs[p, slot : slot + 1, :] * carry + line_sums[k, p, slot_rows(slot), :]
-                )
-            for z in range(Z):
-                result[k, z, slot_rows(slot), :] += along_z[z, slot : slot + 1, :] * enters
+        slot = SLOTS[k]
+        carry = jnp.zeros((PW, S), F32)
+        for z in range(Z) if k % 2 == 0 else range(Z - 1, -1, -1):
+            result[k, z] = carry
+            carry = decs[z, slot : slot + 1, :] * carry + arrived[k, z]
+        line_sums[k, line] = carry
+
+    def compose(k, carry):
+        slot = SLOTS[k]
+        along_z = before_z if k % 2 == 0 else after_z
+        enters = jnp.zeros((PW, S), F32)
+        for p in range(Z) if k % 2 == 0 else range(Z - 1, -1, -1):
+            enters = jnp.where(line == p, carry, enters)
+            carry = line_decs[p, slot : slot + 1, :] * carry + line_sums[k, p]
+        for z in range(Z):
+            result[k, z] += along_z[z, slot : slot + 1, :] * enters
+        return carry
 
     def to_lines(k):
         wait(rems, TO_OWNER + k, arrived.at[k])
@@ -238,9 +224,9 @@
                 line_sums.at[k, line], line_sums.at[k, line], TO_LINES + k, other * Z + pz
             )
 
-    def back(k):
+    def back(k, carry):
         wait(rems, TO_LINES + k, line_sums.at[k])
-        compose(k)
+        carry = compose(k, carry)
         returned[k, pz] = result[k, pz]
 
         def to(z):
@@ -249,6 +235,7 @@
         pl.when(pz != 0)(lambda: to(0))
         for z in z_at:
             pl.when(z != 0)(functools.partial(to, z))
+        return carry
 
     d_cum = [within(0), None]
 
@@ -269,24 +256,19 @@
     to_owners(3)
     to_lines(1)
     to_lines(2)
+    to_lines(3)
     wait(rems, 1, line_decs)
-    back(0)
-    to_lines(3)
-    back(1)
-    back(2)
-    back(3)
+    nothing = jnp.zeros((PW, S), F32)
+    middle = back(0, nothing)
+    back(1, middle)
+    middle = back(2, nothing)
+    back(3, middle)
 
     d_cum[1] = within(1)
 
-    def unpack(first_piece):
-        for part in range(2):
-            wait(rems, BACK + first_piece + part, returned.at[first_piece + part])
-        return [
-            jnp.concatenate(
-                [returned[first_piece + part, :, slot_rows(i), :] for part in range(2)], axis=1
-            ).reshape(W, S)
-            for i in range(2)
-        ]
+    def unpack(k):
+        wait(rems, BACK + k, returned.at[k])
+        return returned[k].reshape(W, S)
 
     after = (row_t >= col_t).astype(F32)
     before = (row_t < col_t).astype(BF16)
@@ -294,9 +276,9 @@
     def along(a, triangle):
         return sum(dot(part, triangle, TN) for part in split(a))
 
-    entering = unpack(0)
-    d_log = []
+    entering, d_log = [], []
     for i in range(2):
+        entering.append(unpack(i))
         parts = split(entering[i])
         carried = rows_mm(cs[i], parts, NT)
         gc_ref[0, i] += rows_mm(gw[i], parts)
@@ -305,14 +287,14 @@
     ends = [
         jnp.concatenate([dec[h, pl.ds(i, 1), 0:1] for h in range(H)], axis=0) for i in range(2)
     ]
-    leaving = unpack(2)
-    for i in range(2):
-        parts = split(leaving[i])
+    for i in (1, 0):
+        leaving = unpack(3 - i)
+        parts = split(leaving)
         weighted = to_end[i] * rows_mm(bs[i], parts, NT)
         gx_ref[0, i] += weighted
         gb_ref[0, i] += rows_mm(xw[i], parts)
         fresh = by_head(x_ref[0, i] * weighted, pick32)
-        product = jnp.sum((leaving[i] * entering[i]).reshape(H, PW, S), axis=1)
+        product = jnp.sum((leaving * entering[i]).reshape(H, PW, S), axis=1)
         through = jnp.sum(product, axis=1, keepdims=True) * ends[i]
         gs_ref[0, i] = -rate * (d_log[i] + along(fresh, before) + through)
 
@@ -340,7 +322,7 @@
     vmem = pl.BlockSpec(memory_space=pltpu.VMEM)
     hbm = pl.BlockSpec(memory_space=pltpu.HBM)
     decays = pltpu.VMEM((8, 2, S), F32)
-    chunks = pltpu.VMEM((PIECES, 8, 2 * PART, S), F32)
+    chunks = pltpu.VMEM((PIECES, 8, PW, S), F32)
     n_sems = 2 + 3 * PIECES
     outs = [jax.ShapeDtypeStruct(a.shape, F32) for a in (inputs, b_matrix, c_matrix, step_sizes)]
     results = pl.pallas_call(

time: 46 us -> 45.5 us (0.989)
  the two profiles are of different devices: /device:TPU:8 before, /device:TPU:1 now
where the time goes in v5:
time: 45.5 us; the launch traced here: 44.8 us
  Pallas kernels  44.1 us (97%)
  between operations  0.64 us (1%)
    pallas_call x1, Pallas kernels, per_device(): pl.pallas_call(kernel, name='mirrored_scan', out_shape=outs, in_specs=[hb...  42.4 us
    pallas_call x1, Pallas kernels, per_device(): pl.pallas_call(leave, name='leave', out_shape=outs, in_specs=[vmem] * 4,...  1.68 us

profile of v5, /device:TPU:1, one launch (start us, length us, event | category | flops | bytes accessed | tf_op | source)
XLA Modules:
  0.0 44.8 jit_solution(8292661211564608902)
XLA Ops:
  0.6 42.4 %mirrored_scan.1 = (f32[1,2,64,256]{3,2,1,0:T(8,128)}, f32[1,2,64,128]{3,2,1,0:T(8,128)}, f32[1,2,64,128]{3,2,1,0:T(8,128)}, f32[1,2,8,64]{3,2,1,0:T(8,128)}) custom-call(f32[1,2,64,256]{3,2,1,0:T(8,128)} %x_any.1, f32[1,2,64,128]{3,2,1,0:T(8,128)} %b_any.1, f32[1,2,64,128]{3,2,1,0:T(8,128)} %c_any.1, f32[1,2,8,64]{3,2,1,0:T(8,128)} %st_any.1, f32[8]{0:T(128)} %rate_any.1, ...), custom_call_target="tpu_custom_call" | custom-call | tf_op jit(solution)/shard_map/mirrored_scan/pallas_call | solution.py:328
  43.1 1.7 %leave.1 = (f32[1,2,64,256]{3,2,1,0:T(8,128)}, f32[1,2,64,128]{3,2,1,0:T(8,128)}, f32[1,2,64,128]{3,2,1,0:T(8,128)}, f32[1,2,8,64]{3,2,1,0:T(8,128)}) custom-call(f32[1,2,64,256]{3,2,1,0:T(8,128)} %get-tuple-element.8.refs_0_, f32[1,2,64,128]{3,2,1,0:T(8,128)} %get-tuple-element.9.refs_1_, f32[1,2,64,128]{3,2,1,0:T(8,128)} %get-tuple-element.10.refs_2_, ...), custom_call_target="tpu_custom_call" | custom-call | tf_op jit(solution)/shard_map/leave/pallas_call | solution.py:348

commit v6 on v5

--- a/solution.py
+++ b/solution.py
@@ -65,7 +65,7 @@
     me = lax.axis_index("ctx")
     line, pz = me // Z, me % Z
     px, py = line // Y, line % Y
-    z_at = [lax.rem(pz + k, Z) for k in (4, 3, 5, 2, 6, 1, 7)]
+    z_at = [lax.rem(pz + k, Z) for k in (4, 5, 3, 6, 2, 7, 1)]
     lines = [
         lax.rem(px + x, X) * Y + lax.rem(py + y, Y) for y in (1, 0) for x in (2, 1, 3, 0)
     ][:-1]
@@ -265,6 +265,11 @@
     back(3, middle)
 
     d_cum[1] = within(1)
+    wait(sems, 0, decs)
+    wait(sems, 1, line_decs)
+    for k in range(PIECES):
+        wait(sems, TO_OWNER + k, outgoing.at[k])
+        wait(sems, TO_LINES + k, line_sums.at[k])
 
     def unpack(k):
         wait(rems, BACK + k, returned.at[k])
@@ -298,11 +303,7 @@
         through = jnp.sum(product, axis=1, keepdims=True) * ends[i]
         gs_ref[0, i] = -rate * (d_log[i] + along(fresh, before) + through)
 
-    wait(sems, 0, decs)
-    wait(sems, 1, line_decs)
     for k in range(PIECES):
-        wait(sems, TO_OWNER + k, outgoing.at[k])
-        wait(sems, TO_LINES + k, line_sums.at[k])
         wait(sems, BACK + k, result.at[k])
 
 

time: 45.5 us -> 45.5 us (level)
  no operation moved by 1% of the time
where the time goes in v6:
time: 45.5 us; the launch traced here: 45 us
  Pallas kernels  44.3 us (97%)
  between operations  0.64 us (1%)
    pallas_call x1, Pallas kernels, per_device(): pl.pallas_call(kernel, name='mirrored_scan', out_shape=outs, in_specs=[hb...  42.7 us
    pallas_call x1, Pallas kernels, per_device(): pl.pallas_call(leave, name='leave', out_shape=outs, in_specs=[vmem] * 4,...  1.68 us

profile of v6, /device:TPU:1, one launch (start us, length us, event | category | flops | bytes accessed | tf_op | source)
XLA Modules:
  0.0 45.0 jit_solution(3131514654160184776)
XLA Ops:
  0.6 42.7 %mirrored_scan.1 = (f32[1,2,64,256]{3,2,1,0:T(8,128)}, f32[1,2,64,128]{3,2,1,0:T(8,128)}, f32[1,2,64,128]{3,2,1,0:T(8,128)}, f32[1,2,8,64]{3,2,1,0:T(8,128)}) custom-call(f32[1,2,64,256]{3,2,1,0:T(8,128)} %x_any.1, f32[1,2,64,128]{3,2,1,0:T(8,128)} %b_any.1, f32[1,2,64,128]{3,2,1,0:T(8,128)} %c_any.1, f32[1,2,8,64]{3,2,1,0:T(8,128)} %st_any.1, f32[8]{0:T(128)} %rate_any.1, ...), custom_call_target="tpu_custom_call" | custom-call | tf_op jit(solution)/shard_map/mirrored_scan/pallas_call | solution.py:329
  43.3 1.7 %leave.1 = (f32[1,2,64,256]{3,2,1,0:T(8,128)}, f32[1,2,64,128]{3,2,1,0:T(8,128)}, f32[1,2,64,128]{3,2,1,0:T(8,128)}, f32[1,2,8,64]{3,2,1,0:T(8,128)}) custom-call(f32[1,2,64,256]{3,2,1,0:T(8,128)} %get-tuple-element.8.refs_0_, f32[1,2,64,128]{3,2,1,0:T(8,128)} %get-tuple-element.9.refs_1_, f32[1,2,64,128]{3,2,1,0:T(8,128)} %get-tuple-element.10.refs_2_, ...), custom_call_target="tpu_custom_call" | custom-call | tf_op jit(solution)/shard_map/leave/pallas_call | solution.py:349

commit v7 on v6

--- a/solution.py
+++ b/solution.py
@@ -67,7 +67,7 @@
     px, py = line // Y, line % Y
     z_at = [lax.rem(pz + k, Z) for k in (4, 5, 3, 6, 2, 7, 1)]
     lines = [
-        lax.rem(px + x, X) * Y + lax.rem(py + y, Y) for y in (1, 0) for x in (2, 1, 3, 0)
+        lax.rem(px + x, X) * Y + lax.rem(py + y, Y) for x in (2, 1, 3, 0) for y in (1, 0)
     ][:-1]
 
     barrier = pltpu.get_barrier_semaphore()

time: 45.5 us -> 45.5 us (level)
  no operation moved by 1% of the time
where the time goes in v7:
time: 45.5 us; the launch traced here: 44.8 us
  Pallas kernels  44.2 us (97%)
  between operations  0.64 us (1%)
    pallas_call x1, Pallas kernels, per_device(): pl.pallas_call(kernel, name='mirrored_scan', out_shape=outs, in_specs=[hb...  42.5 us
    pallas_call x1, Pallas kernels, per_device(): pl.pallas_call(leave, name='leave', out_shape=outs, in_specs=[vmem] * 4,...  1.68 us

profile of v7, /device:TPU:1, one launch (start us, length us, event | category | flops | bytes accessed | tf_op | source)
XLA Modules:
  0.0 44.8 jit_solution(4897107508337521365)
XLA Ops:
  0.6 42.5 %mirrored_scan.1 = (f32[1,2,64,256]{3,2,1,0:T(8,128)}, f32[1,2,64,128]{3,2,1,0:T(8,128)}, f32[1,2,64,128]{3,2,1,0:T(8,128)}, f32[1,2,8,64]{3,2,1,0:T(8,128)}) custom-call(f32[1,2,64,256]{3,2,1,0:T(8,128)} %x_any.1, f32[1,2,64,128]{3,2,1,0:T(8,128)} %b_any.1, f32[1,2,64,128]{3,2,1,0:T(8,128)} %c_any.1, f32[1,2,8,64]{3,2,1,0:T(8,128)} %st_any.1, f32[8]{0:T(128)} %rate_any.1, ...), custom_call_target="tpu_custom_call" | custom-call | tf_op jit(solution)/shard_map/mirrored_scan/pallas_call | solution.py:329
  43.1 1.7 %leave.1 = (f32[1,2,64,256]{3,2,1,0:T(8,128)}, f32[1,2,64,128]{3,2,1,0:T(8,128)}, f32[1,2,64,128]{3,2,1,0:T(8,128)}, f32[1,2,8,64]{3,2,1,0:T(8,128)}) custom-call(f32[1,2,64,256]{3,2,1,0:T(8,128)} %get-tuple-element.8.refs_0_, f32[1,2,64,128]{3,2,1,0:T(8,128)} %get-tuple-element.9.refs_1_, f32[1,2,64,128]{3,2,1,0:T(8,128)} %get-tuple-element.10.refs_2_, ...), custom_call_target="tpu_custom_call" | custom-call | tf_op jit(solution)/shard_map/leave/pallas_call | solution.py:349
